TPU v7x, 32 devices: a whole 2x2x4 slice. The times are simulated.
32 devices in a mesh: row: 2 (over core), col: 16 (over z, y, x).
Axes of the slice: x: 2, y: 2, z: 4, core: 2. Of those that a mesh axis runs over, the one named last changes fastest.
Arguments:
- tile_amps: bfloat16 [6144, 6144], P('row', 'col'), as said below
- cycle_ints: bfloat16 [6144, 6144], P('row', 'col'), as said below
- base_ints: bfloat16 [6144, 6144], P('row', 'col'), as said below
- amp_mask: int32 [96, 96], P('row', 'col'), may hold values from 0 to 1, as said below
- int_mask: int32 [96, 96], P('row', 'col'), may hold values from 0 to 1, as said below
- pair_amps: bfloat16 [64, 196608], P(None, ('row', 'col')), may hold values from -6 to 6
- ladder_ints: bfloat16 [196608, 1024], P(('row', 'col')), may hold values from -0.02734375 to 0.02734375
- pair_list: int32 [16], replicated, may hold values from 0 to 63, as said below
Outputs:
- cycle_residual: float32 [6144, 6144], P('row', 'col')
- ladder: float32 [16, 1024], P(None, 'col')
Inputs may be any that keep to these rules, and one draw needn't show every extreme that they name: `tile_amps`: equal to its transpose. `cycle_ints`: equal to its transpose. `base_ints`: equal to its transpose. `amp_mask`: 0 or 1, equal to its transpose, 1 on every diagonal tile. `int_mask`: 0 or 1, equal to its transpose, 1 on every diagonal tile. `pair_list`: distinct entries.
All inputs are finite; a program needn't handle non-finite values.
Results may differ from a plain program's by a relative error of at most 0.0029.
Values may be sent and summed in bfloat16 or wider, within the bound.
A program may use at most 128 MiB of HBM per device.

v0:
```python
import jax
import jax.numpy as jnp
from jax import lax
from jax.sharding import PartitionSpec as P


def widen(mask, field):
    rows, cols = mask.shape
    tile = field.shape[0] // rows
    spread = jnp.broadcast_to(mask.astype(field.dtype)[:, None, :, None], (rows, tile, cols, tile))
    return field * spread.reshape(rows * tile, cols * tile)


def on_device(
    tile_amps, cycle_ints, base_ints, amp_mask, int_mask, pair_amps, ladder_ints, pair_list
):
    amplitudes = widen(amp_mask, tile_amps)
    integrals = widen(int_mask, cycle_ints)
    baseline = widen(int_mask, base_ints)
    amp_panel = lax.all_gather(amplitudes, "col", axis=1, tiled=True)
    int_columns = lax.all_gather(integrals, "row", axis=0, tiled=True)
    product = jnp.dot(amp_panel, int_columns, preferred_element_type=jnp.float32)
    turned = (baseline.astype(jnp.float32) + product).astype(jnp.bfloat16)
    turned_columns = lax.all_gather(turned, "row", axis=0, tiled=True)
    inter_rows = lax.all_to_all(turned_columns, "col", split_axis=0, concat_axis=1, tiled=True)
    cycle_residual = lax.dot_general(
        amp_panel, inter_rows, (((1,), (1,)), ((), ())), preferred_element_type=jnp.float32
    )
    stored = pair_amps.shape[0]
    selector = (pair_list[:, None] == jnp.arange(stored, dtype=jnp.int32)[None, :]).astype(
        jnp.bfloat16
    )
    chosen = jnp.dot(selector, pair_amps, preferred_element_type=jnp.float32).astype(jnp.bfloat16)
    partial_sums = jnp.dot(chosen, ladder_ints, preferred_element_type=jnp.float32)
    totals = lax.psum(partial_sums, ("row", "col"))
    share_width = totals.shape[1] // lax.axis_size("col")
    ladder = lax.dynamic_slice_in_dim(totals, lax.axis_index("col") * share_width, share_width, 1)
    return (cycle_residual, ladder)


def solution(mesh):
    in_specs = (
        P("row", "col"),
        P("row", "col"),
        P("row", "col"),
        P("row", "col"),
        P("row", "col"),
        P(None, ("row", "col")),
        P(("row", "col"), None),
        P(),
    )
    out_specs = (P("row", "col"), P(None, "col"))
    return jax.shard_map(
        on_device, mesh=mesh, in_specs=in_specs, out_specs=out_specs, check_vma=False
    )
```

profile of v0, /device:TPU:1, one launch (start us, length us, event | category | flops | bytes accessed | tf_op | source)
XLA Modules:
  0.0 712.3 jit_solution(12439366761375615506)
XLA Ops:
  8.0 0.0 copy-start
  8.0 0.0 copy-start.1
  8.0 0.0 all-gather.6.cloned.1.call-start
  8.1 4.4 copy.14
  12.4 0.0 copy-done.1
  12.4 2.9 broadcast_in_dim.5
  15.3 5.8 reshape.18
  21.1 4.0 mul.14
  25.1 0.0 copy-start.2
  25.1 0.0 all-gather.6.cloned.1.call-update
  25.1 0.0 all-gather.4.cloned.1.call-start
  25.2 4.3 copy.12
  29.4 0.0 copy-done.2
  29.5 2.9 broadcast_in_dim.4
  32.3 7.1 reshape.17
  39.4 4.7 mul.12
  44.0 0.0 all-gather.4.cloned.1.call-update
  44.1 0.2 all-gather.8.cloned.1.call-start
  44.3 2.5 copy.13
  46.8 0.0 all-gather.6.cloned.1.call-done
  46.8 389.9 %all-gather.4.cloned.1.call-done = bf16[3072,6144]{0,1:T(8,128)(2,1)} async-done(((bf16[3072,384]{0,1:T(8,128)(2,1)}), bf16[3072,6144]{0,1:T(8,128)(2,1)}) %all-gather.4.cloned.1.call-update) | async-done | bytes 37748752 | tf_op jit(solution)/shard_map/all_gather | solution.py:20
  436.6 27.9 %add_convert_fusion = bf16[3072,384]{1,0:T(8,128)(2,1)} fusion(bf16[3072,6144]{0,1:T(8,128)(2,1)} %all-gather.4.cloned.1.call-done, bf16[6144,384]{0,1:T(8,128)(2,1)} %all-gather.6.cloned.1.call-done, bf16[3072,384]{1,0:T(8,128)(2,1)} %param.10, bf16[3072,384]{1,0:T(8,128)(2,1)} %copy.13), kind=kOutput, calls=%fused_computation.1 | convolution fusion | flops 14500233216 | bytes 49545216 | tf_op jit(solution)/shard_map/dot_general | solution.py:22
  464.5 0.0 all-gather.8.cloned.1.call-update
  464.5 13.6 %all-gather.8.cloned.1.call-done = bf16[6144,384]{1,0:T(8,128)(2,1)} async-done(((bf16[3072,384]{1,0:T(8,128)(2,1)}), bf16[6144,384]{1,0:T(8,128)(2,1)}) %all-gather.8.cloned.1.call-update) | async-done | bytes 4718608 | tf_op jit(solution)/shard_map/all_gather | solution.py:24
  478.1 6.6 copy.15
  484.7 0.0 copy-start.3
  484.7 6.8 all-to-all-start
  491.5 0.0 all-reduce.2.cloned.1.call-start
  491.5 0.0 copy-done
  491.6 0.0 copy-done.3
  491.6 6.3 fusion
  497.9 0.0 all-reduce.2.cloned.1.call-update
  497.9 179.6 %all-reduce.2.cloned.1.call-done = f32[16,1024]{1,0:T(8,128)} async-done(((f32[16,1024]{1,0:T(8,128)}), f32[16,1024]{1,0:T(8,128)}) %all-reduce.2.cloned.1.call-update) | async-done | bytes 65552 | tf_op jit(solution)/shard_map/psum | solution.py:35
  677.5 1.4 constant_dynamic-slice_fusion
  678.9 0.0 all-to-all-done
  678.9 26.3 %fusion.3 = f32[3072,384]{1,0:T(8,128)} fusion(bf16[3072,6144]{0,1:T(8,128)(2,1)} %all-gather.4.cloned.1.call-done, bf16[384,6144]{0,1:T(8,128)(2,1)} %bitcast.2), kind=kOutput, calls=%fused_computation.6 | convolution fusion | flops 14495514624 | bytes 47185920 | tf_op jit(solution)/shard_map/dot_general | solution.py:26
  (2 shorter events, 0.0 us)
Async XLA Ops:
  8.0 483.5 %copy-start = (bf16[64,6144]{1,0:T(8,128)(2,1)S(1)}, bf16[64,6144]{1,0:T(8,128)(2,1)}, u32[]{:S(2)}) copy-start(bf16[64,6144]{1,0:T(8,128)(2,1)} %param.13) | copy-start | bytes 2359300
  8.0 4.4 copy-start.1
  8.0 38.7 %all-gather.6.cloned.1.call-start = ((), (), s32[]{:S(2)}) async-start(), calls=%async_computation.2 | async-start | bytes 7077888 | tf_op jit(solution)/shard_map/all_gather | solution.py:21
  25.1 4.4 copy-start.2
  25.1 411.5 %all-gather.4.cloned.1.call-start = ((), (), s32[]{:S(2)}) async-start(), calls=%async_computation.1 | async-start | bytes 40108032 | tf_op jit(solution)/shard_map/all_gather | solution.py:20
  44.1 434.0 %all-gather.8.cloned.1.call-start = ((), (), s32[]{:S(2)}) async-start(), calls=%async_computation.3 | async-start | bytes 7077888 | tf_op jit(solution)/shard_map/all_gather | solution.py:24
  484.7 6.8 copy-start.3
  484.7 194.2 %all-to-all-start = ((bf16[16,384,384]{1,2,0:T(8,128)(2,1)}), bf16[16,384,384]{1,2,0:T(8,128)(2,1)}, u32[]{:S(2)}, u32[]{:S(2)}) async-start(bf16[16,384,384]{1,2,0:T(8,128)(2,1)} %copy.15), calls=%async_computation | async-start | bytes 9437184 | tf_op jit(solution)/shard_map/all_to_all | solution.py:25
  491.5 186.0 %all-reduce.2.cloned.1.call-start = ((), (), s32[]{:S(2)}) async-start(), calls=%async_computation.4 | async-start | bytes 131072 | tf_op jit(solution)/shard_map/psum | solution.py:35
Sparse Core Ops, SparseCore 0:
  25.2 16.8 all-gather.5
  45.5 391.0 all-gather.3
  464.6 13.4 all-gather.7
Sparse Core Ops, SparseCore 1:
  498.0 179.5 all-reduce.1
where the time goes:
time: 713 us; the launch traced here: 712 us
  waiting for transfers between devices  583 us (82%)
  matrix products  60.5 us (8%)
  local copies, waits for them, and re-layouts  37.6 us (5%)
  between operations  15.3 us (2%)
  other arithmetic  8.71 us (1%)
    all_gather x1, waiting for transfers between devices, on_device(): amp_panel = lax.all_gather(amplitudes, 'col', axis=1, tiled=True)  390 us
    psum x1, waiting for transfers between devices, on_device(): totals = lax.psum(partial_sums, ('row', 'col'))  180 us
    dot_general x1, matrix products, on_device(): jnp.dot(amp_panel, int_columns, preferred_element_type=jnp.float32)  27.9 us
    dot_general x1, matrix products, on_device(): lax.dot_general(amp_panel, inter_rows, (((1,), (1,)), ((), ())), preferre...  26.3 us
    reshape x3, local copies, waits for them, and re-layouts, widen(): return field * spread.reshape(rows * tile, cols * tile)  15.3 us
  transfers between devices with their start and end apart: 5, of which 3 were waited for; matrix products, arithmetic and copies ran while one was open for 4% of the time, Pallas kernels for 0%

commit v1 on v0

v1 whole, which is shorter than its diff:
```python
import functools

import jax
import jax.numpy as jnp
from jax import lax
from jax.experimental import pallas as pl
from jax.experimental.pallas import tpu as pltpu
from jax.sharding import PartitionSpec as P

SMEM = pltpu.SMEM
VMEM = pltpu.VMEM
MIB = 1024 * 1024


def widen(mask, field):
    rows, cols = mask.shape
    tile = field.shape[0] // rows
    spread = jnp.broadcast_to(mask.astype(field.dtype)[:, None, :, None], (rows, tile, cols, tile))
    return field * spread.reshape(rows * tile, cols * tile)


def pack_kernel(tile, cap, sel_ref, mask_ref, field_ref, other_ref, out_ref, ids_ref, masked_ref):
    rows, cols = sel_ref.shape
    high = lax.broadcasted_iota(jnp.int32, (tile, 2 * tile), 1) >= tile

    def row(p, count):
        span = pl.ds(pl.multiple_of(p * tile, tile), tile)
        masked_ref[span, :] = other_ref[span, :]
        for c in range(cols):
            lanes = slice(c * tile, (c + 1) * tile)

            @pl.when(mask_ref[p, c] == 0)
            def _():
                masked_ref[span, lanes] = jnp.zeros((tile, tile), masked_ref.dtype)

            chosen = sel_ref[p, c]

            @pl.when((chosen != 0) & (count < cap))
            def _():
                one = field_ref[span, lanes]
                both = jnp.concatenate([one, one], axis=1)
                slot = count // 2
                keep = high | (count % 2 == 0)
                out_ref[slot] = jnp.where(keep, both, out_ref[slot])
                ids_ref[count] = p * 256 + c
                ids_ref[count + 1] = p * 256 + c

            count = count + chosen
        return count

    ids_ref[ids_ref.shape[0] - 1] = lax.fori_loop(0, rows, row, jnp.int32(0))


def pack(tile, cap, length, sel, mask, field, other):
    return pl.pallas_call(
        functools.partial(pack_kernel, tile, cap),
        out_shape=(
            jax.ShapeDtypeStruct((cap // 2, tile, 2 * tile), field.dtype),
            jax.ShapeDtypeStruct((length,), jnp.int32),
            jax.ShapeDtypeStruct(other.shape, other.dtype),
        ),
        in_specs=[
            pl.BlockSpec(memory_space=SMEM),
            pl.BlockSpec(memory_space=SMEM),
            pl.BlockSpec(memory_space=VMEM),
            pl.BlockSpec(memory_space=VMEM),
        ],
        out_specs=(
            pl.BlockSpec(memory_space=VMEM),
            pl.BlockSpec(memory_space=SMEM),
            pl.BlockSpec(memory_space=VMEM),
        ),
        compiler_params=pltpu.CompilerParams(vmem_limit_bytes=24 * MIB),
        name="pack_tiles",
    )(sel, mask, field, other)


def multiply_kernel(tile, cols, span, place_ref, ids_ref, packed_ref, x_ref, *rest):
    if len(rest) == 5:
        base_ref, out_ref, panel, slots, sems = rest
    else:
        base_ref = None
        out_ref, panel, slots, sems = rest
    senders, pairs = packed_ref.shape[:2]
    height, width = panel.shape
    rows = height // tile
    tiles = width // tile
    last = ids_ref.shape[1] - 1
    place = place_ref[0]
    high = lax.broadcasted_iota(jnp.int32, (tile, 2 * tile), 1) // tile

    def fetch(sender):
        return pltpu.make_async_copy(
            packed_ref.at[sender], slots.at[sender % 2], sems.at[sender % 2]
        )

    fetch(0).start()

    @pl.loop(0, rows)
    def _(p):
        panel[pl.ds(pl.multiple_of(p * tile, tile), tile), :] = jnp.zeros(
            (tile, width), panel.dtype
        )

    def put(a, b, both):
        where_rows = pl.ds(pl.multiple_of(a * tile, tile), tile)
        where_cols = pl.ds(pl.multiple_of((b // 2) * (2 * tile), 2 * tile), 2 * tile)
        keep = high == b % 2
        panel[where_rows, where_cols] = jnp.where(keep, both, panel[where_rows, where_cols])

    @pl.loop(0, senders)
    def _(sender):
        fetch(sender).wait()

        @pl.when(sender + 1 < senders)
        def _():
            fetch(sender + 1).start()

        first = sender * cols - place * rows
        first = jnp.where(first < 0, first + tiles, first)
        count = jnp.minimum(ids_ref[sender, last], 2 * pairs)
        used = (count + 1) // 2
        buffer = slots.at[sender % 2]

        def straight(i):
            ida = ids_ref[sender, 2 * i]
            idb = ids_ref[sender, 2 * i + 1]
            pair = buffer[i]
            left = pair[:, :tile]
            right = pair[:, tile:]
            pa, qa = ida // 256, first + ida % 256
            pb, qb = idb // 256, first + idb % 256
            put(pa, qa, jnp.concatenate([left, left], axis=1))
            put(pb, qb, jnp.concatenate([right, right], axis=1))
            return pair, pa, qa, pb, qb

        @pl.when(first < rows)
        def _():
            @pl.loop(0, used)
            def _(i):
                pair, pa, qa, pb, qb = straight(i)
                turned = jnp.concatenate([pair, pair], axis=0).T
                put(qa, pa, turned[:tile])
                put(qb, pb, turned[tile:])

        @pl.when(first >= rows)
        def _():
            @pl.loop(0, used)
            def _(i):
                straight(i)

    @pl.loop(0, height // span)
    def _(m):
        band = pl.ds(pl.multiple_of(m * span, span), span)
        total = jnp.dot(panel[band, :], x_ref[...], preferred_element_type=jnp.float32)
        if base_ref is not None:
            total = total + base_ref[band, :].astype(jnp.float32)
        out_ref[band, :] = total.astype(out_ref.dtype)


def multiply(tile, cols, rows, place, ids, packed, x, base, dtype):
    height, width = rows * tile, x.shape[0]
    span = next(s for s in (512, 256, 128, tile) if height % s == 0)
    operands = [place, ids, packed, x] + ([] if base is None else [base])
    smem, vmem = pl.BlockSpec(memory_space=SMEM), pl.BlockSpec(memory_space=VMEM)
    in_specs = [smem, smem, pl.BlockSpec(memory_space=pl.ANY), vmem] + ([] if base is None else [vmem])
    return pl.pallas_call(
        functools.partial(multiply_kernel, tile, cols, span),
        out_shape=jax.ShapeDtypeStruct((height, x.shape[1]), dtype),
        in_specs=in_specs,
        out_specs=vmem,
        scratch_shapes=[
            pltpu.VMEM((height, width), x.dtype),
            pltpu.VMEM((2,) + packed.shape[1:], packed.dtype),
            pltpu.SemaphoreType.DMA((2,)),
        ],
        compiler_params=pltpu.CompilerParams(vmem_limit_bytes=60 * MIB),
        cost_estimate=pl.CostEstimate(
            flops=2 * height * width * x.shape[1], bytes_accessed=packed.size * 2, transcendentals=0
        ),
        name="multiply_tiles",
    )(*operands)


def own_first(block):
    n = lax.axis_size("row")
    parts = [block]
    for shift in range(1, n):
        parts.append(lax.ppermute(block, "row", [((i + shift) % n, i) for i in range(n)]))
    return jnp.concatenate(parts, axis=0)


def on_device(
    tile_amps, cycle_ints, base_ints, amp_mask, int_mask, pair_amps, ladder_ints, pair_list
):
    rows, cols = amp_mask.shape
    tile = tile_amps.shape[0] // rows
    senders = lax.axis_size("col")
    place = lax.axis_index("row")
    cap = rows * cols // 3 if rows * cols >= 256 else rows * cols
    cap += cap % 2
    length = -(-(cap + 1) // 128) * 128

    p = place * rows + jnp.arange(rows, dtype=jnp.int32)[:, None]
    q = lax.axis_index("col") * cols + jnp.arange(cols, dtype=jnp.int32)[None, :]
    odd = (p + q) % 2 == 1
    sent = jnp.where(q // rows == place, jnp.where(p > q, odd, ~odd), True).astype(jnp.int32)

    ints, int_ids, baseline = pack(tile, cap, length, int_mask * sent, int_mask, cycle_ints, base_ints)
    amps, amp_ids, amplitudes = pack(tile, cap, length, amp_mask * sent, amp_mask, tile_amps, tile_amps)
    both_ids = jnp.stack([int_ids, amp_ids])
    all_ids = lax.all_gather(both_ids, ("row", "col"), axis=0, tiled=False)
    fits = jnp.max(all_ids[:, :, length - 1]) <= cap
    row_ids = lax.dynamic_slice_in_dim(all_ids, place * senders, senders, 0)

    stored = pair_amps.shape[0]
    selector = (pair_list[:, None] == jnp.arange(stored, dtype=jnp.int32)[None, :]).astype(
        jnp.bfloat16
    )
    chosen = jnp.dot(selector, pair_amps, preferred_element_type=jnp.float32).astype(jnp.bfloat16)
    partial_sums = jnp.dot(chosen, ladder_ints, preferred_element_type=jnp.float32)

    def packed_way(partial_sums):
        where = place.reshape(1).astype(jnp.int32)
        int_tiles = lax.all_gather(ints, "col", axis=0, tiled=False)
        amp_tiles = lax.all_gather(amps, "col", axis=0, tiled=False)
        totals = lax.psum(partial_sums, ("row", "col"))
        inter = multiply(
            tile, cols, rows, where, row_ids[:, 0], int_tiles, own_first(amplitudes), baseline,
            jnp.bfloat16,
        )
        residual = multiply(
            tile, cols, rows, where, row_ids[:, 1], amp_tiles, own_first(inter), None, jnp.float32
        )
        return residual, totals

    def whole_way(partial_sums):
        integrals = widen(int_mask, cycle_ints)
        amp_panel = lax.all_gather(amplitudes, "col", axis=1, tiled=True)
        int_columns = lax.all_gather(integrals, "row", axis=0, tiled=True)
        product = jnp.dot(amp_panel, int_columns, preferred_element_type=jnp.float32)
        turned = (baseline.astype(jnp.float32) + product).astype(jnp.bfloat16)
        turned_columns = lax.all_gather(turned, "row", axis=0, tiled=True)
        inter_rows = lax.all_to_all(turned_columns, "col", split_axis=0, concat_axis=1, tiled=True)
        residual = lax.dot_general(
            amp_panel, inter_rows, (((1,), (1,)), ((), ())), preferred_element_type=jnp.float32
        )
        return residual, lax.psum(partial_sums, ("row", "col"))

    if rows % cols == 0:
        cycle_residual, totals = lax.cond(fits, packed_way, whole_way, partial_sums)
    else:
        cycle_residual, totals = whole_way(partial_sums)
    share_width = totals.shape[1] // senders
    ladder = lax.dynamic_slice_in_dim(totals, lax.axis_index("col") * share_width, share_width, 1)
    return (cycle_residual, ladder)


def solution(mesh):
    in_specs = (
        P("row", "col"),
        P("row", "col"),
        P("row", "col"),
        P("row", "col"),
        P("row", "col"),
        P(None, ("row", "col")),
        P(("row", "col"), None),
        P(),
    )
    out_specs = (P("row", "col"), P(None, "col"))
    return jax.shard_map(
        on_device, mesh=mesh, in_specs=in_specs, out_specs=out_specs, check_vma=False
    )
```

time: 713 us -> 612 us (0.86)
  waiting for transfers between devices: 583 us -> 349 us
  Pallas kernels: 0 us -> 151 us
  blocking collectives: 0 us -> 70.2 us
  matrix products: 60.5 us -> 5.69 us
  local copies, waits for them, and re-layouts: 37.6 us -> 5.85 us
    all_gather x3 -> x2, waiting for transfers between devices: 403 us -> 217 us  [the longest x1 139 us: packed_way(): int_tiles = lax.all_gather(ints, 'col', axis=0, tiled=False)]
    pallas_call x0 -> x4, Pallas kernels: none -> 151 us  [the longest x2 132 us: multiply(): pl.pallas_call(functools.partial(multiply_kernel, tile, cols, span), out_...]
    all_gather x0 -> x1, blocking collectives: none -> 70.2 us  [on_device(): all_ids = lax.all_gather(both_ids, ('row', 'col'), axis=0, tiled=False)]
    psum x1, waiting for transfers between devices: 180 us -> 123 us  [whole_way(): return (residual, lax.psum(partial_sums, ('row', 'col')))]
    dot_general x2 -> x0, matrix products: 54.2 us -> none  [the longest x1 27.9 us: on_device(): jnp.dot(amp_panel, int_columns, preferred_element_type=jnp.float32)]
    reshape x3 -> x0, local copies, waits for them, and re-layouts: 15.3 us -> none  [widen(): return field * spread.reshape(rows * tile, cols * tile)]
    concatenate x0 -> x2, other arithmetic: none -> 9.75 us  [own_first(): return jnp.concatenate(parts, axis=0)]
    mul x2 -> x1, other arithmetic: 8.7 us -> 0.09 us  [on_device(): int_mask * sent]
  transfers between devices with their start and end apart: 5 -> 5, of which waited for: 3 -> 5; matrix products, arithmetic and copies ran while one was open for 4% -> 2% of each run, Pallas kernels for 0% -> 11%
where the time goes in v1:
time: 612 us
  waiting for transfers between devices  349 us (57%)
  Pallas kernels  151 us (25%)
  blocking collectives  70.2 us (11%)
  between operations  16.2 us (3%)
  other arithmetic  10.6 us (2%)
    all_gather x1, waiting for transfers between devices, packed_way(): int_tiles = lax.all_gather(ints, 'col', axis=0, tiled=False)  139 us
    pallas_call x2, Pallas kernels, multiply(): pl.pallas_call(functools.partial(multiply_kernel, tile, cols, span), out_...  132 us
    psum x1, waiting for transfers between devices, whole_way(): return (residual, lax.psum(partial_sums, ('row', 'col')))  123 us
    all_gather x1, waiting for transfers between devices, packed_way(): amp_tiles = lax.all_gather(amps, 'col', axis=0, tiled=False)  77.8 us
    all_gather x1, blocking collectives, on_device(): all_ids = lax.all_gather(both_ids, ('row', 'col'), axis=0, tiled=False)  70.2 us
    pallas_call x2, Pallas kernels, pack(): pl.pallas_call(functools.partial(pack_kernel, tile, cap), out_shape=(jax....  18.9 us
  transfers between devices with their start and end apart: 5, of which 5 were waited for; matrix products, arithmetic and copies ran while one was open for 2% of the time, Pallas kernels for 11%

profile of v1, /device:TPU:1, one launch (start us, length us, event | category | flops | bytes accessed | tf_op | source)
XLA Modules:
  0.0 611.7 jit_solution(8924497615645642064)
XLA Ops:
  8.0 0.0 copy-start
  8.1 0.8 copy.29.mask_ref
  8.9 0.8 copy.31.mask_ref
  9.7 0.1 broadcast_select_fusion.1
  9.8 0.0 copy-start.2
  9.8 1.7 copy-done.2
  11.4 0.0 copy-start.3
  11.4 0.0 copy-start.4
  11.4 0.0 copy-start.9
  11.4 10.0 %pack_tiles.3 = (bf16[48,64,128]{2,1,0:T(8,128)(2,1)}, s32[128]{0:T(128)S(1)}, bf16[3072,384]{1,0:T(8,128)(2,1)}) custom-call(s32[48,6]{1,0:T(8,128)S(1)} %get-tuple-element.113.sel_ref, s32[48,6]{1,0:T(8,128)S(1)} %copy.31.mask_ref, bf16[3072,384]{1,0:T(8,128)(2,1)S(1)} %copy-done.2, bf16[3072,384]{1,0:T(8,128)(2,1)S(1)} %copy-done.2), custom_call_target="tpu_custom_call" | custom-call | tf_op jit(solution)/shard_map/pack_tiles/pallas_call | solution.py:55
  21.4 0.0 copy-done.3
  21.4 0.0 copy-done.4
  21.4 8.9 %pack_tiles.2 = (bf16[48,64,128]{2,1,0:T(8,128)(2,1)}, s32[128]{0:T(128)S(1)}, bf16[3072,384]{1,0:T(8,128)(2,1)}) custom-call(s32[48,6]{1,0:T(8,128)S(1)} %get-tuple-element.112.sel_ref, s32[48,6]{1,0:T(8,128)S(1)} %copy.29.mask_ref, bf16[3072,384]{1,0:T(8,128)(2,1)S(1)} %copy-done.4, bf16[3072,384]{1,0:T(8,128)(2,1)S(1)} %copy-done.3), custom_call_target="tpu_custom_call" | custom-call | tf_op jit(solution)/shard_map/pack_tiles/pallas_call | solution.py:55
  30.4 70.2 %all-gather.3 = s32[32,2,128]{2,1,0:T(2,128)S(1)} all-gather(s32[1,2,128]{2,1,0:T(2,128)S(1)} %add_bitcast_fusion), channel_id=4, replica_groups=mesh['row'=2,'col'=16] {'row','col'}, dimensions={0}, use_global_device_ids=true | all-gather | bytes 33792 | tf_op jit(solution)/shard_map/all_gather | solution.py:212
  100.6 0.7 slice_reduce_fusion
  102.0 0.0 copy-done
  102.0 0.0 copy-done.9
  102.0 0.0 copy-start.8
  102.0 5.7 fusion.1
  107.7 0.0 copy-done.8
  107.7 371.9 %conditional.1 = (f32[3072,384]{1,0:T(8,128)}, f32[16,1024]{1,0:T(8,128)S(1)}) conditional(s32[]{:T(128)} %convert_element_type.17, (bf16[3072,384]{1,0:T(8,128)(2,1)}, s32[48,6]{0,1:T(8,128)S(1)}, bf16[3072,384]{1,0:T(8,128)(2,1)}, bf16[3072,384]{1,0:T(8,128)(2,1)}, f32[16,1024]{1,0:T(8,128)S(1)}) %tuple.50, (s32[]{:T(128)}, ...), branch_computations={%region_1.3_spmd, %region_3.5_spmd} | conditional | flops 29009903616 | bytes 318507392 | solution.py:251
  107.9 0.0 all-gather.18.cloned.1.call-start
  108.0 0.7 all-gather.18.cloned.1.call-update
  108.6 0.0 all-gather.16.cloned.1.call-start
  108.7 0.7 all-gather.16.cloned.1.call-update
  109.4 1.3 collective-permute-start
  110.7 0.6 dynamic-slice_bitcast_fusion
  111.3 0.0 copy-start.6
  111.3 3.9 collective-permute-done
  115.2 5.5 pad_maximum_fusion.x_ref
  120.7 138.9 %all-gather.18.cloned.1.call-done = bf16[768,64,128]{2,1,0:T(8,128)(2,1)} async-done(((bf16[48,64,128]{2,1,0:T(8,128)(2,1)}), bf16[768,64,128]{2,1,0:T(8,128)(2,1)}) %all-gather.18.cloned.1.call-update) | async-done | bytes 12582928 | tf_op jit(solution)/shard_map/cond/branch_1_fun/all_gather | solution.py:225
  259.6 0.0 copy-done.6
  259.6 65.1 %multiply_tiles.2 = bf16[3072,384]{1,0:T(8,128)(2,1)} custom-call(s32[1]{0:T(128)} %bitcast.4.place_ref, s32[16,128]{1,0:T(8,128)} %get-tuple-element.110.ids_ref, bf16[16,48,64,128]{3,2,1,0:T(8,128)(2,1)} %bitcast.40, bf16[6144,384]{1,0:T(8,128)(2,1)} %pad_maximum_fusion.x_ref, bf16[3072,384]{1,0:T(8,128)(2,1)S(1)} %copy-done.6), custom_call_target="tpu_custom_call" | custom-call | flops 14495514624 | bytes 12582912 | tf_op jit(solution)/shard_map/cond/branch_1_fun/multiply_tiles/pallas_call | solution.py:167
  324.8 1.6 collective-permute-start.1
  326.4 4.4 collective-permute-done.1
  330.8 4.2 pad_maximum_fusion.1.x_ref
  335.0 77.8 %all-gather.16.cloned.1.call-done = bf16[768,64,128]{2,1,0:T(8,128)(2,1)} async-done(((bf16[48,64,128]{2,1,0:T(8,128)(2,1)}), bf16[768,64,128]{2,1,0:T(8,128)(2,1)}) %all-gather.16.cloned.1.call-update) | async-done | bytes 12582928 | tf_op jit(solution)/shard_map/cond/branch_1_fun/all_gather | solution.py:226
  412.8 66.9 %multiply_tiles.3 = f32[3072,384]{1,0:T(8,128)} custom-call(s32[1]{0:T(128)} %bitcast.4.place_ref, s32[16,128]{1,0:T(8,128)} %get-tuple-element.111.ids_ref, bf16[16,48,64,128]{3,2,1,0:T(8,128)(2,1)} %bitcast.39, bf16[6144,384]{1,0:T(8,128)(2,1)} %pad_maximum_fusion.1.x_ref), custom_call_target="tpu_custom_call" | custom-call | flops 14495514624 | bytes 12582912 | tf_op jit(solution)/shard_map/cond/branch_1_fun/multiply_tiles/pallas_call | solution.py:167
  479.7 0.0 copy-start.7
  479.7 0.0 copy-start.1
  479.7 0.0 all-reduce.2.cloned.1.call-start
  479.7 0.5 copy-done.7
  480.3 0.0 all-reduce.2.cloned.1.call-update
  480.3 122.6 %all-reduce.2.cloned.1.call-done = f32[16,1024]{1,0:T(8,128)} async-done(((f32[16,1024]{1,0:T(8,128)}), f32[16,1024]{1,0:T(8,128)}) %all-reduce.2.cloned.1.call-update) | async-done | bytes 65552 | tf_op jit(solution)/shard_map/cond/branch_0_fun/psum | solution.py:248
  602.9 1.4 constant_dynamic-slice_fusion
  604.3 0.0 copy-done.1
  (5 shorter events, 0.0 us)
Async XLA Ops:
  8.0 94.0 %copy-start = (bf16[64,6144]{1,0:T(8,128)(2,1)S(1)}, bf16[64,6144]{1,0:T(8,128)(2,1)}, u32[]{:S(2)}) copy-start(bf16[64,6144]{1,0:T(8,128)(2,1)} %param.15) | copy-start | bytes 2359300
  9.8 1.7 copy-start.2
  11.4 10.0 %copy-start.3 = (bf16[3072,384]{1,0:T(8,128)(2,1)S(1)}, bf16[3072,384]{1,0:T(8,128)(2,1)}, u32[]{:S(2)}) copy-start(bf16[3072,384]{1,0:T(8,128)(2,1)} %other_ref.2) | copy-start | bytes 7077892
  11.4 10.0 %copy-start.4 = (bf16[3072,384]{1,0:T(8,128)(2,1)S(1)}, bf16[3072,384]{1,0:T(8,128)(2,1)}, u32[]{:S(2)}) copy-start(bf16[3072,384]{1,0:T(8,128)(2,1)} %field_ref.2) | copy-start | bytes 7077892
  11.4 90.6 %copy-start.9 = (s32[16]{0:T(128)S(1)}, s32[16]{0:T(128)}, u32[]{:S(2)}) copy-start(s32[16]{0:T(128)} %param.17) | copy-start | bytes 196
  102.0 5.7 copy-start.8
  107.9 151.7 %all-gather.18.cloned.1.call-start = ((), (), s32[]{:S(2)}) async-start(), calls=%async_computation.5 | async-start | bytes 13369344 | tf_op jit(solution)/shard_map/cond/branch_1_fun/all_gather | solution.py:225
  108.6 304.1 %all-gather.16.cloned.1.call-start = ((), (), s32[]{:S(2)}) async-start(), calls=%async_computation.4 | async-start | bytes 13369344 | tf_op jit(solution)/shard_map/cond/branch_1_fun/all_gather | solution.py:226
  109.4 5.8 collective-permute-start
  111.3 148.3 %copy-start.6 = (bf16[3072,384]{1,0:T(8,128)(2,1)S(1)}, bf16[3072,384]{1,0:T(8,128)(2,1)}, u32[]{:S(2)}) copy-start(bf16[3072,384]{1,0:T(8,128)(2,1)} %get-tuple-element.46.rest_0_) | copy-start | bytes 7077892 | tf_op jit(solution)/shard_map/cond
  324.8 6.0 collective-permute-start.1
  479.7 0.6 copy-start.7
  479.7 124.6 %copy-start.1 = (bf16[64,6144]{1,0:T(8,128)(2,1)S(1)}, bf16[64,6144]{1,0:T(8,128)(2,1)}, u32[]{:S(2)}) copy-start(bf16[64,6144]{1,0:T(8,128)(2,1)} %param.15) | copy-start | bytes 2359300
  479.7 123.2 %all-reduce.2.cloned.1.call-start = ((), (), s32[]{:S(2)}) async-start(), calls=%async_computation.6 | async-start | bytes 131072 | tf_op jit(solution)/shard_map/cond/branch_0_fun/psum | solution.py:248
Sparse Core Ops, SparseCore 0:
  111.5 148.0 all-gather.17
  262.4 150.3 all-gather.15
Sparse Core Ops, SparseCore 1:
  485.8 117.1 all-reduce.1
